TPU v7x, 512 devices: a whole 4x8x8 slice. The times are simulated.
512 devices in a mesh: ev: 64 (over x, z, core), st: 8 (over y).
Axes of the slice: x: 4, y: 8, z: 8, core: 2. Of those that a mesh axis runs over, the one named last changes fastest.
Arguments:
- waveforms: bfloat16 [2048, 32, 3, 2048], P(('ev', 'st'))
- pair_list: int32 [64, 64, 3], P('ev'), may hold values from 0 to 31, as said below
- pair_count: int32 [64], P('ev'), may hold values from 1 to 64, as said below
Outputs:
- correlation: float32 [4096, 32, 3, 256], P('ev', 'st')
Inputs may be any that keep to these rules, and one draw needn't show every extreme that they name: `pair_list`: each entry holds an event number of 0 to 31 in its first and third place and a block offset o of 0 to 2 in its second, with b + o < 64 for block b; when o is 0 the two events differ. Slots from pair_count onward hold the same law and are ignored. `pair_count`: some block has all 64 slots live in every draw; loads differ widely between blocks.
All inputs are finite; a program needn't handle non-finite values.
Results may differ from a plain program's by a relative error of at most 0.0047.
Values may be sent and summed in bfloat16 or wider, within the bound.
A program may use at most 64 MiB of HBM per device.

v0:
```python
import math

import jax
import jax.numpy as jnp
from jax import lax
from jax.sharding import PartitionSpec as P

LAG = 128
REACH = 2


def passed_along(shard, axis, by):
    devices = lax.axis_size(axis)
    pairs = [(i, i + by) for i in range(devices) if 0 <= i + by < devices]
    return lax.ppermute(shard, axis, pairs)


def base_tables(length):
    doubled = 2 * length
    block_size = min(128, length)
    sample_ids = lax.broadcasted_iota(jnp.int32, (length, block_size), 0)
    column_ids = lax.broadcasted_iota(jnp.int32, (length, block_size), 1)
    phases = sample_ids * column_ids % doubled
    angles = phases.astype(jnp.float32) * (2.0 * math.pi / doubled)
    return (jnp.cos(angles), jnp.sin(angles))


def spectra_of(windows, base):
    base_cos, base_sin = base
    layout = windows.shape
    length = layout[-1]
    doubled = 2 * length
    block_size = base_cos.shape[1]
    turn_total = length // block_size
    flat_rows = windows.reshape(-1, length)
    squares = jnp.mean(jnp.square(flat_rows.astype(jnp.float32)), axis=1)
    scaling = 1.0 / jnp.sqrt(length * (squares + 1e-06))
    sample_ids = lax.broadcasted_iota(jnp.int32, (length, 1), 0)

    def one_turn(turn):
        start_phase = sample_ids * (turn * block_size) % doubled
        start_angle = start_phase.astype(jnp.float32) * (2.0 * math.pi / doubled)
        start_cos = jnp.cos(start_angle)
        start_sin = jnp.sin(start_angle)
        table_cos = start_cos * base_cos - start_sin * base_sin
        table_sin = start_sin * base_cos + start_cos * base_sin
        dft_table = jnp.concatenate([table_cos, -table_sin], axis=1).astype(jnp.bfloat16)
        product = (
            jnp.dot(flat_rows, dft_table, preferred_element_type=jnp.float32) * scaling[:, None]
        )
        return product.astype(jnp.bfloat16)

    pieces = lax.map(one_turn, jnp.arange(turn_total, dtype=jnp.int32))
    pieces = pieces.reshape(turn_total, flat_rows.shape[0], 2, block_size)
    joined = jnp.transpose(pieces, (1, 2, 0, 3)).reshape(flat_rows.shape[0], 2, length)
    return joined.reshape(layout[:-1] + (2, length))


def lag_tables(freqs, spread):
    doubled = 2 * freqs
    frequency = lax.broadcasted_iota(jnp.int32, (freqs, 2 * spread), 0)
    lag_ids = lax.broadcasted_iota(jnp.int32, (freqs, 2 * spread), 1) - spread + doubled
    phases = frequency * lag_ids % doubled
    angles = phases.astype(jnp.float32) * (2.0 * math.pi / doubled)
    weight = jnp.where(frequency == 0, 1.0, 2.0) * (math.sqrt(freqs) / doubled)
    lag_cos = (weight * jnp.cos(angles)).astype(jnp.bfloat16)
    lag_sin = (-weight * jnp.sin(angles)).astype(jnp.bfloat16)
    return (lag_cos, lag_sin)


def shards(waveforms, pair_list, pair_count):
    base = base_tables(waveforms.shape[-1])
    arrived = lax.all_to_all(waveforms, "st", split_axis=1, concat_axis=0, tiled=True)
    own_spec = spectra_of(arrived, base)
    later_items = []
    for offset_step in range(REACH):
        later_items.append(passed_along(own_spec, "ev", -(offset_step + 1)))
    sources = [own_spec] + later_items
    freqs = own_spec.shape[-1]
    lag_cos, lag_sin = lag_tables(freqs, LAG)
    slots = pair_list[0]
    live_count = pair_count[0]
    slot_total = slots.shape[0]
    block_size = min(16, slot_total)
    result = jnp.zeros((slot_total, own_spec.shape[1], own_spec.shape[2], 2 * LAG), jnp.float32)

    def pair_block(turn, result):
        first_slot = turn * block_size
        chosen = lax.dynamic_slice_in_dim(slots, first_slot, block_size, 0)
        first_event = chosen[:, 0]
        block_offset = chosen[:, 1]
        second_event = chosen[:, 2]
        first_spec = own_spec[first_event]
        second_spec = sources[0][second_event]
        for offset_step in range(1, REACH + 1):
            picked = sources[offset_step][second_event]
            second_spec = jnp.where(
                (block_offset == offset_step)[:, None, None, None, None], picked, second_spec
            )
        left_real = first_spec[..., 0, :].astype(jnp.float32)
        left_imag = first_spec[..., 1, :].astype(jnp.float32)
        right_real = second_spec[..., 0, :].astype(jnp.float32)
        right_imag = second_spec[..., 1, :].astype(jnp.float32)
        cross_real = (left_real * right_real + left_imag * right_imag).astype(jnp.bfloat16)
        cross_imag = (left_imag * right_real - left_real * right_imag).astype(jnp.bfloat16)
        lagged = jnp.dot(cross_real.reshape(-1, freqs), lag_cos, preferred_element_type=jnp.float32)
        lagged = lagged + jnp.dot(
            cross_imag.reshape(-1, freqs), lag_sin, preferred_element_type=jnp.float32
        )
        lagged = lagged.reshape(block_size, result.shape[1], result.shape[2], 2 * LAG)
        live_slots = first_slot + lax.broadcasted_iota(jnp.int32, (block_size,), 0) < live_count
        lagged = jnp.where(live_slots[:, None, None, None], lagged, jnp.zeros_like(lagged))
        return lax.dynamic_update_slice_in_dim(result, lagged, first_slot, 0)

    block_count = (live_count + block_size - 1) // block_size
    return lax.fori_loop(0, block_count, pair_block, result)


def solution(mesh):
    in_specs = (P(("ev", "st"), None, None, None), P("ev", None, None), P("ev"))
    out_specs = P("ev", "st", None, None)
    return jax.shard_map(shards, mesh=mesh, in_specs=in_specs, out_specs=out_specs, check_vma=False)
```

profile of v0, /device:TPU:1, one launch (start us, length us, event | category | flops | bytes accessed | tf_op | source)
XLA Modules:
  0.0 526.9 jit_solution(3514574256092106473)
XLA Ops:
  3.8 7.7 %all-to-all-start = ((bf16[4,32,3,2048]{3,0,2,1:T(4,128)(2,1)}), bf16[4,32,3,2048]{3,0,2,1:T(4,128)(2,1)S(1)}, u32[]{:S(2)}, u32[]{:S(2)}) async-start(bf16[4,32,3,2048]{3,0,2,1:T(4,128)(2,1)} %copy.41), calls=%async_computation | async-start | bytes 3145728 | tf_op jit(solution)/shard_map/all_to_all | solution.py:73
  11.4 40.4 %all-to-all-done = bf16[4,32,3,2048]{3,0,2,1:T(4,128)(2,1)S(1)} async-done(((bf16[4,32,3,2048]{3,0,2,1:T(4,128)(2,1)}), bf16[4,32,3,2048]{3,0,2,1:T(4,128)(2,1)S(1)}, u32[]{:S(2)}, u32[]{:S(2)}) %all-to-all-start) | async-done | bytes 1572896 | tf_op jit(solution)/shard_map/all_to_all | solution.py:73
  57.0 5.2 reshape.94
  62.5 133.2 %while.26 = (s32[]{:T(128)}, bf16[16,384,256]{1,2,0:T(8,128)(2,1)S(1)}, s32[16]{0:T(128)S(1)}, bf16[384,2048]{1,0:T(8,128)(2,1)}, f32[384]{0:T(512)S(1)}, /*index=5*/s32[]{:T(128)}, s32[1]{0:T(128)}) while((s32[]{:T(128)}, bf16[16,384,256]{1,2,0:T(8,128)(2,1)S(1)}, s32[16]{0:T(128)S(1)}, bf16[384,2048]{1,0:T(8,128)(2,1)}, ...), condition=%wide.region_2.3_spmd.clone.clone, body=%wide.region_1.2_spmd.clone.clone.sunk | while | flops 411004928 | bytes 3917933 | solution.py:53
  211.9 61.9 %collective-permute-done = bf16[32,4,3,2,2048]{4,3,2,1,0:T(2,128)(2,1)} collective-permute-done((bf16[32,4,3,2,2048]{4,3,2,1,0:T(2,128)(2,1)S(1)}, bf16[32,4,3,2,2048]{4,3,2,1,0:T(2,128)(2,1)}, u32[]{:S(2)}, u32[]{:S(2)}) %collective-permute-start) | collective-permute-done | bytes 3145760 | tf_op jit(solution)/shard_map/ppermute | solution.py:15
  273.8 6.2 %copy.45 = bf16[32,4,3,2,2048]{4,1,3,2,0:T(4,128)(2,1)} copy(bf16[32,4,3,2,2048]{4,3,2,1,0:T(2,128)(2,1)} %collective-permute-done) | data formatting | bytes 6291456
  279.9 28.6 %collective-permute-done.1 = bf16[32,4,3,2,2048]{4,3,2,1,0:T(2,128)(2,1)} collective-permute-done((bf16[32,4,3,2,2048]{4,3,2,1,0:T(2,128)(2,1)S(1)}, bf16[32,4,3,2,2048]{4,3,2,1,0:T(2,128)(2,1)}, u32[]{:S(2)}, u32[]{:S(2)}) %collective-permute-start.1) | collective-permute-done | bytes 3145760 | tf_op jit(solution)/shard_map/ppermute | solution.py:15
  308.5 6.2 %copy.46 = bf16[32,4,3,2,2048]{4,1,3,2,0:T(4,128)(2,1)} copy(bf16[32,4,3,2,2048]{4,3,2,1,0:T(2,128)(2,1)} %collective-permute-done.1) | data formatting | bytes 6291456
  315.7 210.0 %while.27 = (s32[]{:T(128)}, f32[64,4,3,256]{3,1,2,0:T(4,128)}, s32[]{:T(128)}, s32[]{:T(128)}, s32[64,3]{0,1:T(4,128)S(1)}, /*index=5*/bf16[32,4,3,2,2048]{4,1,...) while((s32[]{:T(128)}, f32[64,4,3,256]{3,1,2,0:T(4,128)}, ...), condition=%wide.region_4.5_spmd.clone.clone, body=%wide.region_3.4_spmd.clone.clone.sunk | while | flops 425822368 | bytes 39546244 | solution.py:116
  345.2 4.9 gather_fusion.2
  350.1 6.8 %copy_select_fusion.3 = bf16[16,4,3,2,2048]{4,0,3,2,1:T(8,128)(2,1)S(1)} fusion(bf16[16,4,3,2,2048]{4,1,3,2,0:T(4,128)(2,1)} %gather_fusion, bf16[16,4,3,2,2048]{4,1,3,2,0:T(4,128)(2,1)S(1)} %gather_fusion.1, bf16[16,4,3,2,2048]{4,1,3,2,0:T(4,128)(2,1)} %gather_fusion.2, pred[16]{0:T(512)(128)(4,1)S(1)} %get-tuple-element.444, ...), kind=kLoop, calls=%fused_computation.58.clone.1 | loop fusion | flops 1572864 | bytes 6291488 | tf_op jit(solution)/shard_map/while/body/jit(_where)/select_n | solution.py:97
  365.0 7.8 %fusion.79 = f32[192,256]{1,0:T(8,128)S(1)} fusion(bf16[192,2048]{1,0:T(8,128)(2,1)S(1)} %convert_element_type.248, s32[256]{0:T(256)S(1)} %get-tuple-element.510, f32[2048]{0:T(1024)S(1)} %get-tuple-element.511), kind=kOutput, calls=%fused_computation.61.clone.1 | convolution fusion | flops 209715200 | bytes 992256 | tf_op jit(solution)/shard_map/while/body/dot_general | solution.py:106
  374.2 7.9 %convolution_add_fusion.2 = f32[192,256]{1,0:T(8,128)S(1)} fusion(f32[192,256]{1,0:T(8,128)S(1)} %fusion.79, bf16[192,2048]{1,0:T(8,128)(2,1)S(1)} %convert_element_type.249, f32[2048]{0:T(1024)S(1)} %get-tuple-element.512, s32[256]{0:T(256)S(1)} %get-tuple-element.510), kind=kOutput, calls=%fused_computation.60.clone.1 | convolution fusion | flops 209764352 | bytes 1188864 | tf_op jit(solution)/shard_map/while/body/dot_general | solution.py:107
  392.5 4.9 gather_fusion.2
  397.4 6.8 %copy_select_fusion.3 = bf16[16,4,3,2,2048]{4,0,3,2,1:T(8,128)(2,1)S(1)} fusion(bf16[16,4,3,2,2048]{4,1,3,2,0:T(4,128)(2,1)} %gather_fusion, bf16[16,4,3,2,2048]{4,1,3,2,0:T(4,128)(2,1)S(1)} %gather_fusion.1, bf16[16,4,3,2,2048]{4,1,3,2,0:T(4,128)(2,1)} %gather_fusion.2, pred[16]{0:T(512)(128)(4,1)S(1)} %get-tuple-element.444, ...), kind=kLoop, calls=%fused_computation.58.clone.1 | loop fusion | flops 1572864 | bytes 6291488 | tf_op jit(solution)/shard_map/while/body/jit(_where)/select_n | solution.py:97
  412.2 7.8 %fusion.79 = f32[192,256]{1,0:T(8,128)S(1)} fusion(bf16[192,2048]{1,0:T(8,128)(2,1)S(1)} %convert_element_type.248, s32[256]{0:T(256)S(1)} %get-tuple-element.510, f32[2048]{0:T(1024)S(1)} %get-tuple-element.511), kind=kOutput, calls=%fused_computation.61.clone.1 | convolution fusion | flops 209715200 | bytes 992256 | tf_op jit(solution)/shard_map/while/body/dot_general | solution.py:106
  421.5 7.9 %convolution_add_fusion.2 = f32[192,256]{1,0:T(8,128)S(1)} fusion(f32[192,256]{1,0:T(8,128)S(1)} %fusion.79, bf16[192,2048]{1,0:T(8,128)(2,1)S(1)} %convert_element_type.249, f32[2048]{0:T(1024)S(1)} %get-tuple-element.512, s32[256]{0:T(256)S(1)} %get-tuple-element.510), kind=kOutput, calls=%fused_computation.60.clone.1 | convolution fusion | flops 209764352 | bytes 1188864 | tf_op jit(solution)/shard_map/while/body/dot_general | solution.py:107
  444.6 6.8 %copy_select_fusion.3 = bf16[16,4,3,2,2048]{4,0,3,2,1:T(8,128)(2,1)S(1)} fusion(bf16[16,4,3,2,2048]{4,1,3,2,0:T(4,128)(2,1)} %gather_fusion, bf16[16,4,3,2,2048]{4,1,3,2,0:T(4,128)(2,1)S(1)} %gather_fusion.1, bf16[16,4,3,2,2048]{4,1,3,2,0:T(4,128)(2,1)} %gather_fusion.2, pred[16]{0:T(512)(128)(4,1)S(1)} %get-tuple-element.444, ...), kind=kLoop, calls=%fused_computation.58.clone.1 | loop fusion | flops 1572864 | bytes 6291488 | tf_op jit(solution)/shard_map/while/body/jit(_where)/select_n | solution.py:97
  459.5 7.8 %fusion.79 = f32[192,256]{1,0:T(8,128)S(1)} fusion(bf16[192,2048]{1,0:T(8,128)(2,1)S(1)} %convert_element_type.248, s32[256]{0:T(256)S(1)} %get-tuple-element.510, f32[2048]{0:T(1024)S(1)} %get-tuple-element.511), kind=kOutput, calls=%fused_computation.61.clone.1 | convolution fusion | flops 209715200 | bytes 992256 | tf_op jit(solution)/shard_map/while/body/dot_general | solution.py:106
  468.7 7.9 %convolution_add_fusion.2 = f32[192,256]{1,0:T(8,128)S(1)} fusion(f32[192,256]{1,0:T(8,128)S(1)} %fusion.79, bf16[192,2048]{1,0:T(8,128)(2,1)S(1)} %convert_element_type.249, f32[2048]{0:T(1024)S(1)} %get-tuple-element.512, s32[256]{0:T(256)S(1)} %get-tuple-element.510), kind=kOutput, calls=%fused_computation.60.clone.1 | convolution fusion | flops 209764352 | bytes 1188864 | tf_op jit(solution)/shard_map/while/body/dot_general | solution.py:107
  486.9 4.9 gather_fusion.2
  491.8 6.8 %copy_select_fusion.3 = bf16[16,4,3,2,2048]{4,0,3,2,1:T(8,128)(2,1)S(1)} fusion(bf16[16,4,3,2,2048]{4,1,3,2,0:T(4,128)(2,1)} %gather_fusion, bf16[16,4,3,2,2048]{4,1,3,2,0:T(4,128)(2,1)S(1)} %gather_fusion.1, bf16[16,4,3,2,2048]{4,1,3,2,0:T(4,128)(2,1)} %gather_fusion.2, pred[16]{0:T(512)(128)(4,1)S(1)} %get-tuple-element.444, ...), kind=kLoop, calls=%fused_computation.58.clone.1 | loop fusion | flops 1572864 | bytes 6291488 | tf_op jit(solution)/shard_map/while/body/jit(_where)/select_n | solution.py:97
  506.7 7.8 %fusion.79 = f32[192,256]{1,0:T(8,128)S(1)} fusion(bf16[192,2048]{1,0:T(8,128)(2,1)S(1)} %convert_element_type.248, s32[256]{0:T(256)S(1)} %get-tuple-element.510, f32[2048]{0:T(1024)S(1)} %get-tuple-element.511), kind=kOutput, calls=%fused_computation.61.clone.1 | convolution fusion | flops 209715200 | bytes 992256 | tf_op jit(solution)/shard_map/while/body/dot_general | solution.py:106
  515.9 7.9 %convolution_add_fusion.2 = f32[192,256]{1,0:T(8,128)S(1)} fusion(f32[192,256]{1,0:T(8,128)S(1)} %fusion.79, bf16[192,2048]{1,0:T(8,128)(2,1)S(1)} %convert_element_type.249, f32[2048]{0:T(1024)S(1)} %get-tuple-element.512, s32[256]{0:T(256)S(1)} %get-tuple-element.510), kind=kOutput, calls=%fused_computation.60.clone.1 | convolution fusion | flops 209764352 | bytes 1188864 | tf_op jit(solution)/shard_map/while/body/dot_general | solution.py:107
  (177 shorter events, 231.7 us)
Async XLA Ops:
  3.8 48.1 %all-to-all-start = ((bf16[4,32,3,2048]{3,0,2,1:T(4,128)(2,1)}), bf16[4,32,3,2048]{3,0,2,1:T(4,128)(2,1)S(1)}, u32[]{:S(2)}, u32[]{:S(2)}) async-start(bf16[4,32,3,2048]{3,0,2,1:T(4,128)(2,1)} %copy.41), calls=%async_computation | async-start | bytes 3145728 | tf_op jit(solution)/shard_map/all_to_all | solution.py:73
  57.0 5.5 %copy-start.1 = (bf16[16,384,256]{1,2,0:T(8,128)(2,1)S(1)}, bf16[16,384,256]{1,2,0:T(8,128)(2,1)}, u32[]{:S(2)}) copy-start(bf16[16,384,256]{1,2,0:T(8,128)(2,1)} %custom-call.8) | copy-start | bytes 9437188
  199.2 8.4 %copy-start.2 = (s32[1,64,3]{1,0,2:T(1,128)S(1)}, s32[1,64,3]{1,0,2:T(1,128)}, u32[]{:S(2)}) copy-start(s32[1,64,3]{1,0,2:T(1,128)} %param.8) | copy-start | bytes 2308
  203.0 70.8 %collective-permute-start = (bf16[32,4,3,2,2048]{4,3,2,1,0:T(2,128)(2,1)S(1)}, bf16[32,4,3,2,2048]{4,3,2,1,0:T(2,128)(2,1)}, u32[]{:S(2)}, u32[]{:S(2)}) collective-permute-start(bf16[32,4,3,2,2048]{4,3,2,1,0:T(2,128)(2,1)S(1)} %reshape_reshape.3), channel_id=1, source_target_pairs={{16,0},{24,8},{32,16},{40,24},{48,32},{56,40},{64,48},{72,56},{80,... | collective-permute-start | bytes 9437192 | tf_op jit(solution)/shard_map/ppermute | solution.py:15
  204.3 104.2 %collective-permute-start.1 = (bf16[32,4,3,2,2048]{4,3,2,1,0:T(2,128)(2,1)S(1)}, bf16[32,4,3,2,2048]{4,3,2,1,0:T(2,128)(2,1)}, u32[]{:S(2)}, u32[]{:S(2)}) collective-permute-start(bf16[32,4,3,2,2048]{4,3,2,1,0:T(2,128)(2,1)S(1)} %reshape_reshape.3), channel_id=1, source_target_pairs={{8,0},{16,8},{24,16},{32,24},{40,32},{48,40},{56,48},{64,56},{72,6... | collective-permute-start | bytes 9437192 | tf_op jit(solution)/shard_map/ppermute | solution.py:15
  365.0 7.9 %copy-start = (bf16[16,4,3,1,2048]{4,0,3,2,1:T(8,128)(2,1)S(1)}, bf16[16,4,3,1,2048]{4,0,3,2,1:T(8,128)(2,1)}, u32[]{:S(2)}) copy-start(bf16[16,4,3,1,2048]{4,0,3,2,1:T(8,128)(2,1)} %get-tuple-element.450) | copy-start | bytes 2359300 | tf_op jit(solution)/shard_map/while
  412.2 7.9 %copy-start = (bf16[16,4,3,1,2048]{4,0,3,2,1:T(8,128)(2,1)S(1)}, bf16[16,4,3,1,2048]{4,0,3,2,1:T(8,128)(2,1)}, u32[]{:S(2)}) copy-start(bf16[16,4,3,1,2048]{4,0,3,2,1:T(8,128)(2,1)} %get-tuple-element.450) | copy-start | bytes 2359300 | tf_op jit(solution)/shard_map/while
  459.5 7.9 %copy-start = (bf16[16,4,3,1,2048]{4,0,3,2,1:T(8,128)(2,1)S(1)}, bf16[16,4,3,1,2048]{4,0,3,2,1:T(8,128)(2,1)}, u32[]{:S(2)}) copy-start(bf16[16,4,3,1,2048]{4,0,3,2,1:T(8,128)(2,1)} %get-tuple-element.450) | copy-start | bytes 2359300 | tf_op jit(solution)/shard_map/while
  506.7 7.9 %copy-start = (bf16[16,4,3,1,2048]{4,0,3,2,1:T(8,128)(2,1)S(1)}, bf16[16,4,3,1,2048]{4,0,3,2,1:T(8,128)(2,1)}, u32[]{:S(2)}) copy-start(bf16[16,4,3,1,2048]{4,0,3,2,1:T(8,128)(2,1)} %get-tuple-element.450) | copy-start | bytes 2359300 | tf_op jit(solution)/shard_map/while
where the time goes:
time: 534 us; the launch traced here: 527 us
  local copies, waits for them, and re-layouts  133 us (25%)
  waiting for transfers between devices  131 us (25%)
  other arithmetic  118 us (22%)
  matrix products  98.4 us (18%)
  loops' own time  32.2 us (6%)
  starting transfers between devices  11.6 us (2%)
    ppermute x2, waiting for transfers between devices, passed_along(): return lax.ppermute(shard, axis, pairs)  90.5 us
    another operation x16, other arithmetic  75.9 us
    all_to_all x1, waiting for transfers between devices, shards(): lax.all_to_all(waveforms, 'st', split_axis=1, concat_axis=0, tiled=True)  40.4 us
    gather x8, local copies, waits for them, and re-layouts, pair_block(): picked = sources[offset_step][second_event]  38.8 us
    dot_general x16, matrix products, one_turn(): jnp.dot(flat_rows, dft_table, preferred_element_type=jnp.float32)  35.5 us
    dot_general x4, matrix products, pair_block(): jnp.dot(cross_imag.reshape(-1, freqs), lag_sin, preferred_element_type=jn...  31.6 us
    dot_general x4, matrix products, pair_block(): jnp.dot(cross_real.reshape(-1, freqs), lag_cos, preferred_element_type=jn...  31.3 us
    select_n x4, other arithmetic, pair_block(): jnp.where((block_offset == offset_step)[:, None, None, None, None], picke...  27.4 us
  transfers between devices with their start and end apart: 3, of which 3 were waited for; matrix products, arithmetic and copies ran while one was open for 2% of the time, Pallas kernels for 0%

commit v1 on v0

v1 whole, which is shorter than its diff:
```python
import math

import jax
import jax.numpy as jnp
import numpy as np
from jax import lax
from jax.experimental import pallas as pl
from jax.experimental.pallas import tpu as pltpu
from jax.sharding import PartitionSpec as P

MESH = pl.DeviceIdType.MESH
EV, ST = 64, 8
EVENTS, OWN, STATIONS, COMP, WIN = 32, 4, 4, 3, 2048
PAIRS, LAGS = 64, 256
HALF, CHUNK, SIZE = 1024, 256, 512
STEPS = HALF // CHUNK
ROWS = EVENTS * 8
PART = OWN * 8
PIECES = 2 * COMP
WINDOW = 2
ORDER = (4, 3, 5, 2, 6, 1, 7)
ARRIVAL = (1, 7, 2, 6, 3, 5, 4)


def tables():
    sample = np.arange(SIZE)[:, None]
    odd = 2 * np.arange(SIZE // 2)[None, :] + 1
    angle = (sample * odd % (2 * SIZE)) * (math.pi / SIZE)
    forward = np.concatenate([np.cos(angle), -np.sin(angle)], axis=1)
    weight = 2.0 / SIZE * math.sqrt(WIN)
    back = weight * forward[:LAGS].T
    return jnp.asarray(forward, jnp.bfloat16), jnp.asarray(back, jnp.bfloat16)


def upper(shape, axis):
    return lax.broadcasted_iota(jnp.int32, shape, axis) < 4


def swap_halves(value):
    return pltpu.roll(value, 4, 1)


def kernel(
    slots_ref, count_ref, wave_ref, forward_hbm, back_hbm, out_ref,
    forward_ref, back_ref, raw, parts, held, wide, first_spec, second_spec, nyquist, scales, adder, cross, rank_one,
    table_sem, raw_sem, own_sem, y_send, y_recv, z_send, z_recv, s_send, s_recv,
):
    ev = lax.axis_index("ev")
    st = lax.axis_index("st")
    core = lax.rem(ev, 2)
    earlier = lax.rem(ev + EV - 2, EV)
    later = lax.rem(ev + 2, EV)
    sibling = ev + 1 - 2 * core

    raw_copies = []
    for c in range(COMP):
        copy = pltpu.make_async_copy(wave_ref.at[:, c], raw.at[:, c], raw_sem.at[c])
        copy.start()
        raw_copies.append(copy)
    table_copies = [
        pltpu.make_async_copy(forward_hbm, forward_ref, table_sem.at[0]),
        pltpu.make_async_copy(back_hbm, back_ref, table_sem.at[1]),
    ]
    for copy in table_copies:
        copy.start()

    barrier = pltpu.get_barrier_semaphore()
    for by in range(1, ST):
        pl.semaphore_signal(
            barrier, inc=1, device_id=(ev, lax.rem(st + by, ST)), device_id_type=MESH
        )
    for other in (earlier, later, sibling):
        pl.semaphore_signal(barrier, inc=1, device_id=(other, st), device_id_type=MESH)

    def place(n, source):
        half = n % 2 * 16
        return n // 2, pl.ds(pl.multiple_of(source * PART + half, 16), 16), slice(half, half + 16)

    def y_copy(n, by):
        target = lax.rem(st + by, ST)
        c, rows, half = place(n, st)
        return pltpu.make_async_remote_copy(
            src_ref=parts.at[c, target, half],
            dst_ref=held.at[0, c, rows],
            send_sem=y_send.at[n, by],
            recv_sem=y_recv.at[n, by],
            device_id=(ev, target),
            device_id_type=MESH,
        )

    def own_copy(n):
        c, rows, half = place(n, st)
        return pltpu.make_async_copy(parts.at[c, st, half], held.at[0, c, rows], own_sem.at[n])

    def z_copy(n, by):
        c, rows, _ = place(n, lax.rem(st + ST - by, ST))
        return pltpu.make_async_remote_copy(
            src_ref=held.at[0, c, rows],
            dst_ref=held.at[2, c, rows],
            send_sem=z_send.at[n, by],
            recv_sem=z_recv.at[n, by],
            device_id=(earlier, st),
            device_id_type=MESH,
        )

    def sibling_copy(n, by):
        c, rows, _ = place(n, lax.rem(st + ST - by, ST))
        return pltpu.make_async_remote_copy(
            src_ref=held.at[2 - 2 * core, c, rows],
            dst_ref=held.at[1, c, rows],
            send_sem=s_send.at[n, by],
            recv_sem=s_recv.at[n, by],
            device_id=(sibling, st),
            device_id_type=MESH,
        )

    def lay_out(c):
        def group(g, carry):
            stations = pl.ds(pl.multiple_of(g * 16, 16), 16)
            for pair in range(OWN // 2):
                for piece in range(HALF // 256):
                    low = slice(piece * 256, piece * 256 + 256)
                    high = slice(HALF + piece * 256, HALF + piece * 256 + 256)
                    made = [[], [], [], []]
                    for e in (2 * pair, 2 * pair + 1):
                        head = raw[e, c, stations, low].astype(jnp.float32)
                        tail = raw[e, c, stations, high].astype(jnp.float32)
                        for t in range(2):
                            h0 = head[8 * t : 8 * t + 8]
                            h1 = tail[8 * t : 8 * t + 8]
                            top = upper(h0.shape, 0)
                            made[2 * t].append(jnp.where(top, h0, pltpu.roll(h1, 4, 0)))
                            made[2 * t + 1].append(jnp.where(top, pltpu.roll(h0, 4, 0), h1))
                    for d in range(4):
                        both = jnp.concatenate(made[d], axis=0).astype(jnp.bfloat16)
                        parts[c, 4 * g + d, 16 * pair : 16 * pair + 16, low] = both
            return carry

        lax.fori_loop(0, 2, group, 0)

    def measure(c, block):
        energy = jnp.zeros((ROWS, 128), jnp.float32)
        total = jnp.zeros((ROWS, 128), jnp.float32)
        for piece in range(HALF // 128):
            x = held[block, c, :, 128 * piece : 128 * piece + 128].astype(jnp.float32)
            energy = energy + x * x
            total = total + x
        split = []
        for value in (energy, total):
            high = value.astype(jnp.bfloat16)
            wide_high = high.astype(jnp.float32)
            rest = jnp.where(jnp.abs(wide_high) < jnp.inf, value - wide_high, 0.0)
            split += [high, rest.astype(jnp.bfloat16)]
        sums = jnp.dot(
            jnp.concatenate(split, axis=1), adder[...], preferred_element_type=jnp.float32
        ).reshape(EVENTS, 8, 256)
        sums = sums + swap_halves(sums)
        scale = 1.0 / jnp.sqrt(WIN * (sums[:, :, :128] * (1.0 / WIN) + 1e-6))
        scales[block] = scale
        nyquist[pl.ds(block * EVENTS, EVENTS)] = sums[:, :, 128:] * scale

    def scaled(product, block):
        product = product.reshape(EVENTS, 8, SIZE)
        scale = scales[block]
        return jnp.concatenate(
            [product[:, :, 128 * n : 128 * n + 128] * scale for n in range(SIZE // 128)], axis=2
        )

    def transform_first(c):
        x = held[0, c]
        head = swap_halves(x[:, :128].astype(jnp.float32).reshape(EVENTS, 8, 128))
        tail = swap_halves(x[:, HALF - 128 :].astype(jnp.float32).reshape(EVENTS, 8, 128))
        top = upper(head.shape, 1)
        before = jnp.where(top, 0.0, tail).reshape(ROWS, 128).astype(jnp.bfloat16)
        after = jnp.where(top, head, 0.0).reshape(ROWS, 128).astype(jnp.bfloat16)
        wide[:, :128] = before
        wide[:, 128 : 128 + HALF] = x
        wide[:, 128 + HALF :] = after
        for q in range(STEPS):
            product = jnp.dot(
                wide[:, CHUNK * q : CHUNK * q + SIZE],
                forward_ref[...],
                preferred_element_type=jnp.float32,
            )
            first_spec[:, q] = scaled(product, 0)

    def transform_second(c, block):
        for q in range(STEPS):
            product = jnp.dot(
                held[block, c, :, CHUNK * q : CHUNK * q + CHUNK],
                forward_ref[:CHUNK, :],
                preferred_element_type=jnp.float32,
            )
            second_spec[pl.ds(block * EVENTS, EVENTS), q] = scaled(product, block)

    def correlate(c):
        def one(p):
            first = slots_ref[0, 0, p]
            second = slots_ref[1, 0, p] * EVENTS + slots_ref[2, 0, p]
            real = jnp.zeros((8, SIZE // 2), jnp.float32)
            imag = jnp.zeros((8, SIZE // 2), jnp.float32)
            for q in range(STEPS):
                a = first_spec[first, q]
                b = second_spec[second, q]
                ar, ai = a[:, : SIZE // 2], a[:, SIZE // 2 :]
                br, bi = b[:, : SIZE // 2], b[:, SIZE // 2 :]
                real = real + (ar * br + ai * bi)
                imag = imag + (ai * br - ar * bi)
            rank_one[p] = nyquist[first] * nyquist[second]
            return jnp.concatenate([real, imag], axis=1)

        def two(n, carry):
            both = jnp.concatenate([one(2 * n), one(2 * n + 1)], axis=0)
            cross[pl.ds(pl.multiple_of(n * 16, 16), 16), :] = both.astype(jnp.bfloat16)
            return carry

        lax.fori_loop(0, PAIRS // 2, two, 0)
        lagged = jnp.dot(cross[...], back_ref[...], preferred_element_type=jnp.float32)
        lagged = lagged.reshape(PAIRS, 8, LAGS)
        lagged = lagged + swap_halves(lagged)
        odd = lax.rem(lax.broadcasted_iota(jnp.int32, (PAIRS, 8, 128), 2), 2)
        weight = math.sqrt(WIN) / (2 * WIN)
        term = rank_one[...] * jnp.where(odd == 0, weight, -weight)
        lagged = lagged - jnp.concatenate([term, term], axis=2)
        slot = lax.broadcasted_iota(jnp.int32, lagged.shape, 0)
        lagged = jnp.where(slot < count_ref[0], lagged, 0.0)
        out_ref[:, c] = lagged[:, :4]

    def issue(n):
        if n % 2 == 0:
            raw_copies[n // 2].wait()
            lay_out(n // 2)
        if n == 0:
            pl.semaphore_wait(barrier, ST - 1 + 3)
        own_copy(n).start()
        for by in ORDER:
            y_copy(n, by).start()

    def forward(n):
        own_copy(n).wait()
        z_copy(n, 0).start()
        for by in ARRIVAL:
            y_copy(n, by).wait_recv()
            z_copy(n, by).start()

    def share(n):
        for by in (0, *ARRIVAL):
            z_copy(n, by).wait_recv()
            sibling_copy(n, by).start()

    def gather(n):
        for by in range(ST):
            sibling_copy(n, by).wait_recv()

    def compute_own(c):
        measure(c, 0)
        transform_first(c)
        transform_second(c, 0)

    def compute_rest(c):
        gather(2 * c)
        gather(2 * c + 1)
        for block in (2, 1):
            measure(c, block)
            transform_second(c, block)
        correlate(c)

    for n in range(WINDOW):
        issue(n)
    for copy in table_copies:
        copy.wait()
    row = lax.broadcasted_iota(jnp.int32, adder.shape, 0)
    column = lax.broadcasted_iota(jnp.int32, adder.shape, 1)
    sign = 1.0 - 2.0 * lax.rem(row, 2).astype(jnp.float32)
    weight = jnp.where(row < 256, jnp.where(column < 128, 1.0, 0.0), jnp.where(column < 128, 0.0, sign))
    adder[...] = weight.astype(jnp.bfloat16)
    for n in range(PIECES):
        forward(n)
        if n + WINDOW < PIECES:
            issue(n + WINDOW)
        if n:
            share(n - 1)
        if n % 2 == 0 and n:
            compute_rest(n // 2 - 1)
        if n % 2:
            compute_own(n // 2)
    share(PIECES - 1)
    compute_rest(COMP - 1)

    for n in range(PIECES):
        for by in range(ST):
            if by:
                y_copy(n, by).wait_send()
            z_copy(n, by).wait_send()
            sibling_copy(n, by).wait_send()


def shards(waveforms, pair_list, pair_count):
    forward, back = tables()
    windows = jnp.transpose(waveforms, (0, 2, 1, 3))
    slots = jnp.transpose(pair_list, (2, 0, 1))
    whole = pl.BlockSpec(memory_space=pltpu.VMEM)
    scalar = pl.BlockSpec(memory_space=pltpu.SMEM)
    anywhere = pl.BlockSpec(memory_space=pl.ANY)
    dma = pltpu.SemaphoreType.DMA
    result = pl.pallas_call(
        kernel,
        out_shape=jax.ShapeDtypeStruct((PAIRS, COMP, STATIONS, LAGS), jnp.float32),
        in_specs=[scalar, scalar, anywhere, anywhere, anywhere],
        out_specs=whole,
        scratch_shapes=[
            pltpu.VMEM((SIZE, SIZE), jnp.bfloat16),
            pltpu.VMEM((SIZE, LAGS), jnp.bfloat16),
            pltpu.VMEM((OWN, COMP, ST * STATIONS, WIN), jnp.bfloat16),
            pltpu.VMEM((COMP, ST, PART, HALF), jnp.bfloat16),
            pltpu.VMEM((3, COMP, ROWS, HALF), jnp.bfloat16),
            pltpu.VMEM((ROWS, HALF + 256), jnp.bfloat16),
            pltpu.VMEM((EVENTS, STEPS, 8, SIZE), jnp.float32),
            pltpu.VMEM((3 * EVENTS, STEPS, 8, SIZE), jnp.float32),
            pltpu.VMEM((3 * EVENTS, 8, 128), jnp.float32),
            pltpu.VMEM((3, EVENTS, 8, 128), jnp.float32),
            pltpu.VMEM((512, 256), jnp.bfloat16),
            pltpu.VMEM((PAIRS * 8, SIZE), jnp.bfloat16),
            pltpu.VMEM((PAIRS, 8, 128), jnp.float32),
            dma((2,)),
            dma((COMP,)),
            dma((PIECES,)),
            dma((PIECES, ST)),
            dma((PIECES, ST)),
            dma((PIECES, ST)),
            dma((PIECES, ST)),
            dma((PIECES, ST)),
            dma((PIECES, ST)),
        ],
        compiler_params=pltpu.CompilerParams(
            collective_id=0, has_side_effects=True, vmem_limit_bytes=58 * 2**20
        ),
        name="pair_correlation",
    )(slots, pair_count, windows, forward, back)
    return jnp.transpose(result, (0, 2, 1, 3))


def solution(mesh):
    in_specs = (P(("ev", "st"), None, None, None), P("ev", None, None), P("ev"))
    out_specs = P("ev", "st", None, None)
    return jax.shard_map(shards, mesh=mesh, in_specs=in_specs, out_specs=out_specs, check_vma=False)
```

time: 534 us -> 65.1 us (0.12); the launches traced: 527 us -> 64.9 us
  waiting for transfers between devices: 131 us -> 0 us
  local copies, waits for them, and re-layouts: 133 us -> 2.09 us
  other arithmetic: 118 us -> 0 us
  matrix products: 98.4 us -> 0 us
  Pallas kernels: 0 us -> 62.2 us
  loops' own time: 32.2 us -> 0 us
  starting transfers between devices: 11.6 us -> 0 us
    dot_general x24 -> x0, matrix products: 98.4 us -> none  [the longest x16 35.5 us: one_turn(): jnp.dot(flat_rows, dft_table, preferred_element_type=jnp.float32)]
    ppermute x2 -> x0, waiting for transfers between devices: 90.5 us -> none  [passed_along(): return lax.ppermute(shard, axis, pairs)]
    another operation x16 -> x0, other arithmetic: 75.9 us -> none
    gather x16 -> x0, local copies, waits for them, and re-layouts: 69.2 us -> none  [the longest x8 38.8 us: pair_block(): picked = sources[offset_step][second_event]]
    pallas_call x0 -> x1, Pallas kernels: none -> 62.2 us  [shards(): pl.pallas_call(kernel, out_shape=jax.ShapeDtypeStruct((PAIRS, COMP, STATI...]
    all_to_all x1 -> x0, waiting for transfers between devices: 40.4 us -> none  [shards(): lax.all_to_all(waveforms, 'st', split_axis=1, concat_axis=0, tiled=True)]
    another operation x2 -> x0, loops' own time: 32.2 us -> none  [the longest x1 21.4 us: shards(): return lax.fori_loop(0, block_count, pair_block, result)]
    select_n x12 -> x0, other arithmetic: 27.9 us -> none  [the longest x4 27.4 us: pair_block(): jnp.where((block_offset == offset_step)[:, None, None, None, None], picke...]
  transfers between devices with their start and end apart: 3 -> 0, of which waited for: 3 -> 0; matrix products, arithmetic and copies ran while one was open for 2% -> 0% of each run, Pallas kernels for 0% -> 0%
where the time goes in v1:
time: 65.1 us; the launch traced here: 64.9 us
  Pallas kernels  62.2 us (96%)
  local copies, waits for them, and re-layouts  2.09 us (3%)
  between operations  0.66 us (1%)
    pallas_call x1, Pallas kernels, shards(): pl.pallas_call(kernel, out_shape=jax.ShapeDtypeStruct((PAIRS, COMP, STATI...  62.2 us
    unnamed x1, local copies, waits for them, and re-layouts  2.09 us

profile of v1, /device:TPU:1, one launch (start us, length us, event | category | flops | bytes accessed | tf_op | source)
XLA Modules:
  0.0 64.9 jit_solution(6266630813037684562)
XLA Ops:
  0.7 62.2 %pair_correlation.1 = f32[64,3,4,256]{3,2,1,0:T(4,128)} custom-call(s32[3,1,64]{2,1,0:T(1,128)} %bitcast.5, s32[1]{0:T(128)S(6)} %copy.7.count_ref, bf16[4,3,32,2048]{3,2,1,0:T(8,128)(2,1)} %bitcast.4, bf16[512,512]{1,0:T(8,128)(2,1)} %constant.4.clone.forward_hbm, bf16[512,256]{1,0:T(8,128)(2,1)} %constant.5.clone.back_hbm), custom_call_target="tpu_custom_call" | custom-call | tf_op jit(solution)/shard_map/pair_correlation/pallas_call | solution.py:306
  62.8 2.1 %copy.8 = f32[64,4,3,256]{3,1,2,0:T(4,128)} copy(f32[64,4,3,256]{3,1,2,0:T(4,128)} %bitcast.3) | data formatting | bytes 1572864

commit v2 on v1

--- a/solution.py
+++ b/solution.py
@@ -17,9 +17,9 @@
 ROWS = EVENTS * 8
 PART = OWN * 8
 PIECES = 2 * COMP
-WINDOW = 2
+COLUMN = 8
+TOGETHER = 4
 ORDER = (4, 3, 5, 2, 6, 1, 7)
-ARRIVAL = (1, 7, 2, 6, 3, 5, 4)
 
 
 def tables():
@@ -43,7 +43,7 @@
 def kernel(
     slots_ref, count_ref, wave_ref, forward_hbm, back_hbm, out_ref,
     forward_ref, back_ref, raw, parts, held, wide, first_spec, second_spec, nyquist, scales, adder, cross, rank_one,
-    table_sem, raw_sem, own_sem, y_send, y_recv, z_send, z_recv, s_send, s_recv,
+    joined, table_sem, raw_sem, own_sem, y_send, y_recv, z_send, z_recv, s_send, s_recv,
 ):
     ev = lax.axis_index("ev")
     st = lax.axis_index("st")
@@ -65,12 +65,29 @@
         copy.start()
 
     barrier = pltpu.get_barrier_semaphore()
+    first = lax.rem(ev // 2, COLUMN) == 0
+    last = lax.rem(ev // 2, COLUMN) == COLUMN - 1
     for by in range(1, ST):
         pl.semaphore_signal(
             barrier, inc=1, device_id=(ev, lax.rem(st + by, ST)), device_id_type=MESH
         )
-    for other in (earlier, later, sibling):
-        pl.semaphore_signal(barrier, inc=1, device_id=(other, st), device_id_type=MESH)
+    pl.semaphore_signal(barrier, inc=1, device_id=(sibling, st), device_id_type=MESH)
+
+    @pl.when(first)
+    def _():
+        pl.semaphore_signal(barrier, inc=1, device_id=(earlier, st), device_id_type=MESH)
+
+    @pl.when(jnp.logical_not(last))
+    def _():
+        pl.semaphore_signal(barrier, inc=1, device_id=(later, st), device_id_type=MESH)
+
+    def meet():
+        before = jnp.where(first, 0, 1) + jnp.where(last, 1, 0)
+        pl.semaphore_wait(barrier, ST + before)
+
+        @pl.when(last)
+        def _():
+            pl.semaphore_signal(joined, inc=1, device_id=(later, st), device_id_type=MESH)
 
     def place(n, source):
         half = n % 2 * 16
@@ -138,11 +155,18 @@
 
         lax.fori_loop(0, 2, group, 0)
 
-    def measure(c, block):
-        energy = jnp.zeros((ROWS, 128), jnp.float32)
-        total = jnp.zeros((ROWS, 128), jnp.float32)
+    def half_of(c, half, block, lanes):
+        rows = [held[block, c, PART * k + 16 * half : PART * k + 16 * half + 16, lanes] for k in range(ST)]
+        return jnp.concatenate(rows, axis=0)
+
+    def events_of(half, block):
+        return [pl.ds(block * EVENTS + OWN * k + 2 * half, 2) for k in range(ST)]
+
+    def measure(c, half, block):
+        energy = jnp.zeros((ROWS // 2, 128), jnp.float32)
+        total = jnp.zeros((ROWS // 2, 128), jnp.float32)
         for piece in range(HALF // 128):
-            x = held[block, c, :, 128 * piece : 128 * piece + 128].astype(jnp.float32)
+            x = half_of(c, half, block, slice(128 * piece, 128 * piece + 128)).astype(jnp.float32)
             energy = energy + x * x
             total = total + x
         split = []
@@ -153,15 +177,17 @@
             split += [high, rest.astype(jnp.bfloat16)]
         sums = jnp.dot(
             jnp.concatenate(split, axis=1), adder[...], preferred_element_type=jnp.float32
-        ).reshape(EVENTS, 8, 256)
+        ).reshape(EVENTS // 2, 8, 256)
         sums = sums + swap_halves(sums)
         scale = 1.0 / jnp.sqrt(WIN * (sums[:, :, :128] * (1.0 / WIN) + 1e-6))
-        scales[block] = scale
-        nyquist[pl.ds(block * EVENTS, EVENTS)] = sums[:, :, 128:] * scale
-
-    def scaled(product, block):
-        product = product.reshape(EVENTS, 8, SIZE)
-        scale = scales[block]
+        alternate = sums[:, :, 128:] * scale
+        for k, events in enumerate(events_of(half, block)):
+            scales[events] = scale[2 * k : 2 * k + 2]
+            nyquist[events] = alternate[2 * k : 2 * k + 2]
+        return scale
+
+    def scaled(product, scale):
+        product = product.reshape(scale.shape[0], 8, SIZE)
         return jnp.concatenate(
             [product[:, :, 128 * n : 128 * n + 128] * scale for n in range(SIZE // 128)], axis=2
         )
@@ -182,16 +208,19 @@
                 forward_ref[...],
                 preferred_element_type=jnp.float32,
             )
-            first_spec[:, q] = scaled(product, 0)
-
-    def transform_second(c, block):
+            first_spec[:, q] = scaled(product, scales[:EVENTS])
+
+    def transform_second(c, half, block):
+        scale = measure(c, half, block)
         for q in range(STEPS):
             product = jnp.dot(
-                held[block, c, :, CHUNK * q : CHUNK * q + CHUNK],
+                half_of(c, half, block, slice(CHUNK * q, CHUNK * q + CHUNK)),
                 forward_ref[:CHUNK, :],
                 preferred_element_type=jnp.float32,
             )
-            second_spec[pl.ds(block * EVENTS, EVENTS), q] = scaled(product, block)
+            product = scaled(product, scale)
+            for k, events in enumerate(events_of(half, block)):
+                second_spec[events, q] = product[2 * k : 2 * k + 2]
 
     def correlate(c):
         def one(p):
@@ -209,12 +238,13 @@
             rank_one[p] = nyquist[first] * nyquist[second]
             return jnp.concatenate([real, imag], axis=1)
 
-        def two(n, carry):
-            both = jnp.concatenate([one(2 * n), one(2 * n + 1)], axis=0)
-            cross[pl.ds(pl.multiple_of(n * 16, 16), 16), :] = both.astype(jnp.bfloat16)
+        def some(n, carry):
+            made = jnp.concatenate([one(TOGETHER * n + k) for k in range(TOGETHER)], axis=0)
+            rows = pl.ds(pl.multiple_of(n * 8 * TOGETHER, 8 * TOGETHER), 8 * TOGETHER)
+            cross[rows, :] = made.astype(jnp.bfloat16)
             return carry
 
-        lax.fori_loop(0, PAIRS // 2, two, 0)
+        lax.fori_loop(0, PAIRS // TOGETHER, some, 0)
         lagged = jnp.dot(cross[...], back_ref[...], preferred_element_type=jnp.float32)
         lagged = lagged.reshape(PAIRS, 8, LAGS)
         lagged = lagged + swap_halves(lagged)
@@ -231,20 +261,18 @@
             raw_copies[n // 2].wait()
             lay_out(n // 2)
         if n == 0:
-            pl.semaphore_wait(barrier, ST - 1 + 3)
+            meet()
         own_copy(n).start()
         for by in ORDER:
             y_copy(n, by).start()
 
     def forward(n):
-        own_copy(n).wait()
-        z_copy(n, 0).start()
-        for by in ARRIVAL:
+        for by in ORDER:
             y_copy(n, by).wait_recv()
             z_copy(n, by).start()
 
     def share(n):
-        for by in (0, *ARRIVAL):
+        for by in (0, *ORDER):
             z_copy(n, by).wait_recv()
             sibling_copy(n, by).start()
 
@@ -252,21 +280,29 @@
         for by in range(ST):
             sibling_copy(n, by).wait_recv()
 
-    def compute_own(c):
-        measure(c, 0)
-        transform_first(c)
-        transform_second(c, 0)
-
-    def compute_rest(c):
-        gather(2 * c)
-        gather(2 * c + 1)
-        for block in (2, 1):
-            measure(c, block)
-            transform_second(c, block)
-        correlate(c)
-
-    for n in range(WINDOW):
+    def compute_own(n):
+        transform_second(n // 2, n % 2, 0)
+        if n % 2:
+            transform_first(n // 2)
+
+    def compute_rest(n):
+        share(n)
+        transform_second(n // 2, n % 2, 2)
+        gather(n)
+        transform_second(n // 2, n % 2, 1)
+        if n % 2:
+            correlate(n // 2)
+
+    for n in range(PIECES):
         issue(n)
+
+    @pl.when(first)
+    def _():
+        pl.semaphore_wait(joined, 1)
+
+    for n in range(PIECES):
+        own_copy(n).wait()
+        z_copy(n, 0).start()
     for copy in table_copies:
         copy.wait()
     row = lax.broadcasted_iota(jnp.int32, adder.shape, 0)
@@ -276,16 +312,10 @@
     adder[...] = weight.astype(jnp.bfloat16)
     for n in range(PIECES):
         forward(n)
-        if n + WINDOW < PIECES:
-            issue(n + WINDOW)
         if n:
-            share(n - 1)
-        if n % 2 == 0 and n:
-            compute_rest(n // 2 - 1)
-        if n % 2:
-            compute_own(n // 2)
-    share(PIECES - 1)
-    compute_rest(COMP - 1)
+            compute_rest(n - 1)
+        compute_own(n)
+    compute_rest(PIECES - 1)
 
     for n in range(PIECES):
         for by in range(ST):
@@ -318,10 +348,11 @@
             pltpu.VMEM((EVENTS, STEPS, 8, SIZE), jnp.float32),
             pltpu.VMEM((3 * EVENTS, STEPS, 8, SIZE), jnp.float32),
             pltpu.VMEM((3 * EVENTS, 8, 128), jnp.float32),
-            pltpu.VMEM((3, EVENTS, 8, 128), jnp.float32),
+            pltpu.VMEM((3 * EVENTS, 8, 128), jnp.float32),
             pltpu.VMEM((512, 256), jnp.bfloat16),
             pltpu.VMEM((PAIRS * 8, SIZE), jnp.bfloat16),
             pltpu.VMEM((PAIRS, 8, 128), jnp.float32),
+            pltpu.SemaphoreType.REGULAR,
             dma((2,)),
             dma((COMP,)),
             dma((PIECES,)),

time: 65.1 us -> 59.4 us (0.912)
  Pallas kernels: 62.2 us -> 56 us
    pallas_call x1, Pallas kernels: 62.2 us -> 56 us  [shards(): pl.pallas_call(kernel, out_shape=jax.ShapeDtypeStruct((PAIRS, COMP, STATI...]
where the time goes in v2:
time: 59.4 us; the launch traced here: 58.8 us
  Pallas kernels  56 us (94%)
  local copies, waits for them, and re-layouts  2.09 us (4%)
  between operations  0.66 us (1%)
    pallas_call x1, Pallas kernels, shards(): pl.pallas_call(kernel, out_shape=jax.ShapeDtypeStruct((PAIRS, COMP, STATI...  56 us
    unnamed x1, local copies, waits for them, and re-layouts  2.09 us

profile of v2, /device:TPU:1, one launch (start us, length us, event | category | flops | bytes accessed | tf_op | source)
XLA Modules:
  0.0 58.8 jit_solution(3373820096612065600)
XLA Ops:
  0.7 56.0 %pair_correlation.1 = f32[64,3,4,256]{3,2,1,0:T(4,128)} custom-call(s32[3,1,64]{2,1,0:T(1,128)} %bitcast.5, s32[1]{0:T(128)S(6)} %copy.7.count_ref, bf16[4,3,32,2048]{3,2,1,0:T(8,128)(2,1)} %bitcast.4, bf16[512,512]{1,0:T(8,128)(2,1)} %constant.4.clone.forward_hbm, bf16[512,256]{1,0:T(8,128)(2,1)} %constant.5.clone.back_hbm), custom_call_target="tpu_custom_call" | custom-call | tf_op jit(solution)/shard_map/pair_correlation/pallas_call | solution.py:336
  56.7 2.1 %copy.8 = f32[64,4,3,256]{3,1,2,0:T(4,128)} copy(f32[64,4,3,256]{3,1,2,0:T(4,128)} %bitcast.3) | data formatting | bytes 1572864

commit v3 on v2

--- a/solution.py
+++ b/solution.py
@@ -15,7 +15,6 @@
 HALF, CHUNK, SIZE = 1024, 256, 512
 STEPS = HALF // CHUNK
 ROWS = EVENTS * 8
-PART = OWN * 8
 PIECES = 2 * COMP
 COLUMN = 8
 TOGETHER = 4
@@ -42,7 +41,7 @@
 
 def kernel(
     slots_ref, count_ref, wave_ref, forward_hbm, back_hbm, out_ref,
-    forward_ref, back_ref, raw, parts, held, wide, first_spec, second_spec, nyquist, scales, adder, cross, rank_one,
+    forward_ref, back_ref, raw, parts, held, wide, first_spec, second_spec, nyquist, adder, cross, rank_one,
     joined, table_sem, raw_sem, own_sem, y_send, y_recv, z_send, z_recv, s_send, s_recv,
 ):
     ev = lax.axis_index("ev")
@@ -89,45 +88,59 @@
         def _():
             pl.semaphore_signal(joined, inc=1, device_id=(later, st), device_id_type=MESH)
 
-    def place(n, source):
-        half = n % 2 * 16
-        return n // 2, pl.ds(pl.multiple_of(source * PART + half, 16), 16), slice(half, half + 16)
+    def rows_of(source):
+        return pl.ds(pl.multiple_of(source * 16, 16), 16)
 
     def y_copy(n, by):
+        c, half = n // 2, n % 2
         target = lax.rem(st + by, ST)
-        c, rows, half = place(n, st)
         return pltpu.make_async_remote_copy(
             src_ref=parts.at[c, target, half],
-            dst_ref=held.at[0, c, rows],
-            send_sem=y_send.at[n, by],
+            dst_ref=held.at[0, c, half, rows_of(st)],
+            send_sem=y_send.at[n],
             recv_sem=y_recv.at[n, by],
             device_id=(ev, target),
             device_id_type=MESH,
         )
 
     def own_copy(n):
-        c, rows, half = place(n, st)
-        return pltpu.make_async_copy(parts.at[c, st, half], held.at[0, c, rows], own_sem.at[n])
-
-    def z_copy(n, by):
-        c, rows, _ = place(n, lax.rem(st + ST - by, ST))
+        c, half = n // 2, n % 2
+        return pltpu.make_async_copy(
+            parts.at[c, st, half], held.at[0, c, half, rows_of(st)], own_sem.at[n]
+        )
+
+    def z_copy(n, rows):
+        c, half = n // 2, n % 2
         return pltpu.make_async_remote_copy(
-            src_ref=held.at[0, c, rows],
-            dst_ref=held.at[2, c, rows],
-            send_sem=z_send.at[n, by],
-            recv_sem=z_recv.at[n, by],
+            src_ref=held.at[0, c, half, rows],
+            dst_ref=held.at[2, c, half, rows],
+            send_sem=z_send.at[n],
+            recv_sem=z_recv.at[n],
             device_id=(earlier, st),
             device_id_type=MESH,
         )
 
-    def sibling_copy(n, by):
-        c, rows, _ = place(n, lax.rem(st + ST - by, ST))
+    def sibling_copy(n):
+        c, half = n // 2, n % 2
         return pltpu.make_async_remote_copy(
-            src_ref=held.at[2 - 2 * core, c, rows],
-            dst_ref=held.at[1, c, rows],
-            send_sem=s_send.at[n, by],
-            recv_sem=s_recv.at[n, by],
+            src_ref=held.at[2 - 2 * core, c, half],
+            dst_ref=held.at[1, c, half],
+            send_sem=s_send.at[n],
+            recv_sem=s_recv.at[n],
             device_id=(sibling, st),
+            device_id_type=MESH,
+        )
+
+    every = pl.ds(0, 16 * ST)
+
+    def y_sent(n):
+        rows = pl.ds(0, 16 * (ST - 1))
+        return pltpu.make_async_remote_copy(
+            src_ref=held.at[0, n // 2, n % 2, rows],
+            dst_ref=held.at[0, n // 2, n % 2, rows],
+            send_sem=y_send.at[n],
+            recv_sem=y_recv.at[n, 0],
+            device_id=(ev, lax.rem(st + 1, ST)),
             device_id_type=MESH,
         )
 
@@ -150,14 +163,10 @@
                             made[2 * t + 1].append(jnp.where(top, pltpu.roll(h0, 4, 0), h1))
                     for d in range(4):
                         both = jnp.concatenate(made[d], axis=0).astype(jnp.bfloat16)
-                        parts[c, 4 * g + d, 16 * pair : 16 * pair + 16, low] = both
+                        parts[c, 4 * g + d, pair, :, low] = both
             return carry
 
         lax.fori_loop(0, 2, group, 0)
-
-    def half_of(c, half, block, lanes):
-        rows = [held[block, c, PART * k + 16 * half : PART * k + 16 * half + 16, lanes] for k in range(ST)]
-        return jnp.concatenate(rows, axis=0)
 
     def events_of(half, block):
         return [pl.ds(block * EVENTS + OWN * k + 2 * half, 2) for k in range(ST)]
@@ -166,7 +175,7 @@
         energy = jnp.zeros((ROWS // 2, 128), jnp.float32)
         total = jnp.zeros((ROWS // 2, 128), jnp.float32)
         for piece in range(HALF // 128):
-            x = half_of(c, half, block, slice(128 * piece, 128 * piece + 128)).astype(jnp.float32)
+            x = held[block, c, half, :, 128 * piece : 128 * piece + 128].astype(jnp.float32)
             energy = energy + x * x
             total = total + x
         split = []
@@ -182,7 +191,6 @@
         scale = 1.0 / jnp.sqrt(WIN * (sums[:, :, :128] * (1.0 / WIN) + 1e-6))
         alternate = sums[:, :, 128:] * scale
         for k, events in enumerate(events_of(half, block)):
-            scales[events] = scale[2 * k : 2 * k + 2]
             nyquist[events] = alternate[2 * k : 2 * k + 2]
         return scale
 
@@ -192,13 +200,13 @@
             [product[:, :, 128 * n : 128 * n + 128] * scale for n in range(SIZE // 128)], axis=2
         )
 
-    def transform_first(c):
-        x = held[0, c]
-        head = swap_halves(x[:, :128].astype(jnp.float32).reshape(EVENTS, 8, 128))
-        tail = swap_halves(x[:, HALF - 128 :].astype(jnp.float32).reshape(EVENTS, 8, 128))
+    def transform_first(c, half, scale):
+        x = held[0, c, half]
+        head = swap_halves(x[:, :128].astype(jnp.float32).reshape(EVENTS // 2, 8, 128))
+        tail = swap_halves(x[:, HALF - 128 :].astype(jnp.float32).reshape(EVENTS // 2, 8, 128))
         top = upper(head.shape, 1)
-        before = jnp.where(top, 0.0, tail).reshape(ROWS, 128).astype(jnp.bfloat16)
-        after = jnp.where(top, head, 0.0).reshape(ROWS, 128).astype(jnp.bfloat16)
+        before = jnp.where(top, 0.0, tail).reshape(ROWS // 2, 128).astype(jnp.bfloat16)
+        after = jnp.where(top, head, 0.0).reshape(ROWS // 2, 128).astype(jnp.bfloat16)
         wide[:, :128] = before
         wide[:, 128 : 128 + HALF] = x
         wide[:, 128 + HALF :] = after
@@ -208,19 +216,22 @@
                 forward_ref[...],
                 preferred_element_type=jnp.float32,
             )
-            first_spec[:, q] = scaled(product, scales[:EVENTS])
+            product = scaled(product, scale)
+            for k, events in enumerate(events_of(half, 0)):
+                first_spec[events, q] = product[2 * k : 2 * k + 2]
 
     def transform_second(c, half, block):
         scale = measure(c, half, block)
         for q in range(STEPS):
             product = jnp.dot(
-                half_of(c, half, block, slice(CHUNK * q, CHUNK * q + CHUNK)),
+                held[block, c, half, :, CHUNK * q : CHUNK * q + CHUNK],
                 forward_ref[:CHUNK, :],
                 preferred_element_type=jnp.float32,
             )
             product = scaled(product, scale)
             for k, events in enumerate(events_of(half, block)):
                 second_spec[events, q] = product[2 * k : 2 * k + 2]
+        return scale
 
     def correlate(c):
         def one(p):
@@ -269,26 +280,17 @@
     def forward(n):
         for by in ORDER:
             y_copy(n, by).wait_recv()
-            z_copy(n, by).start()
-
-    def share(n):
-        for by in (0, *ORDER):
-            z_copy(n, by).wait_recv()
-            sibling_copy(n, by).start()
-
-    def gather(n):
-        for by in range(ST):
-            sibling_copy(n, by).wait_recv()
+            z_copy(n, rows_of(lax.rem(st + ST - by, ST))).start()
 
     def compute_own(n):
-        transform_second(n // 2, n % 2, 0)
-        if n % 2:
-            transform_first(n // 2)
+        scale = transform_second(n // 2, n % 2, 0)
+        transform_first(n // 2, n % 2, scale)
 
     def compute_rest(n):
-        share(n)
+        z_copy(n, every).wait_recv()
+        sibling_copy(n).start()
         transform_second(n // 2, n % 2, 2)
-        gather(n)
+        sibling_copy(n).wait_recv()
         transform_second(n // 2, n % 2, 1)
         if n % 2:
             correlate(n // 2)
@@ -302,7 +304,7 @@
 
     for n in range(PIECES):
         own_copy(n).wait()
-        z_copy(n, 0).start()
+        z_copy(n, rows_of(st)).start()
     for copy in table_copies:
         copy.wait()
     row = lax.broadcasted_iota(jnp.int32, adder.shape, 0)
@@ -318,11 +320,9 @@
     compute_rest(PIECES - 1)
 
     for n in range(PIECES):
-        for by in range(ST):
-            if by:
-                y_copy(n, by).wait_send()
-            z_copy(n, by).wait_send()
-            sibling_copy(n, by).wait_send()
+        y_sent(n).wait_send()
+        z_copy(n, every).wait_send()
+        sibling_copy(n).wait_send()
 
 
 def shards(waveforms, pair_list, pair_count):
@@ -342,12 +342,11 @@
             pltpu.VMEM((SIZE, SIZE), jnp.bfloat16),
             pltpu.VMEM((SIZE, LAGS), jnp.bfloat16),
             pltpu.VMEM((OWN, COMP, ST * STATIONS, WIN), jnp.bfloat16),
-            pltpu.VMEM((COMP, ST, PART, HALF), jnp.bfloat16),
-            pltpu.VMEM((3, COMP, ROWS, HALF), jnp.bfloat16),
-            pltpu.VMEM((ROWS, HALF + 256), jnp.bfloat16),
+            pltpu.VMEM((COMP, ST, 2, 16, HALF), jnp.bfloat16),
+            pltpu.VMEM((3, COMP, 2, 16 * ST, HALF), jnp.bfloat16),
+            pltpu.VMEM((ROWS // 2, HALF + 256), jnp.bfloat16),
             pltpu.VMEM((EVENTS, STEPS, 8, SIZE), jnp.float32),
             pltpu.VMEM((3 * EVENTS, STEPS, 8, SIZE), jnp.float32),
-            pltpu.VMEM((3 * EVENTS, 8, 128), jnp.float32),
             pltpu.VMEM((3 * EVENTS, 8, 128), jnp.float32),
             pltpu.VMEM((512, 256), jnp.bfloat16),
             pltpu.VMEM((PAIRS * 8, SIZE), jnp.bfloat16),
@@ -356,12 +355,12 @@
             dma((2,)),
             dma((COMP,)),
             dma((PIECES,)),
+            dma((PIECES,)),
             dma((PIECES, ST)),
-            dma((PIECES, ST)),
-            dma((PIECES, ST)),
-            dma((PIECES, ST)),
-            dma((PIECES, ST)),
-            dma((PIECES, ST)),
+            dma((PIECES,)),
+            dma((PIECES,)),
+            dma((PIECES,)),
+            dma((PIECES,)),
         ],
         compiler_params=pltpu.CompilerParams(
             collective_id=0, has_side_effects=True, vmem_limit_bytes=58 * 2**20

time: 59.4 us -> 58.2 us (0.980)
  Pallas kernels: 56 us -> 54.9 us
    pallas_call x1, Pallas kernels: 56 us -> 54.9 us  [shards(): pl.pallas_call(kernel, out_shape=jax.ShapeDtypeStruct((PAIRS, COMP, STATI...]
where the time goes in v3:
time: 58.2 us; the launch traced here: 57.6 us
  Pallas kernels  54.9 us (94%)
  local copies, waits for them, and re-layouts  2.09 us (4%)
  between operations  0.66 us (1%)
    pallas_call x1, Pallas kernels, shards(): pl.pallas_call(kernel, out_shape=jax.ShapeDtypeStruct((PAIRS, COMP, STATI...  54.9 us
    unnamed x1, local copies, waits for them, and re-layouts  2.09 us

profile of v3, /device:TPU:1, one launch (start us, length us, event | category | flops | bytes accessed | tf_op | source)
XLA Modules:
  0.0 57.6 jit_solution(5222387964055781693)
XLA Ops:
  0.7 54.9 %pair_correlation.1 = f32[64,3,4,256]{3,2,1,0:T(4,128)} custom-call(s32[3,1,64]{2,1,0:T(1,128)} %bitcast.5, s32[1]{0:T(128)S(6)} %copy.7.count_ref, bf16[4,3,32,2048]{3,2,1,0:T(8,128)(2,1)} %bitcast.4, bf16[512,512]{1,0:T(8,128)(2,1)} %constant.4.clone.forward_hbm, bf16[512,256]{1,0:T(8,128)(2,1)} %constant.5.clone.back_hbm), custom_call_target="tpu_custom_call" | custom-call | tf_op jit(solution)/shard_map/pair_correlation/pallas_call | solution.py:336
  55.5 2.1 %copy.8 = f32[64,4,3,256]{3,1,2,0:T(4,128)} copy(f32[64,4,3,256]{3,1,2,0:T(4,128)} %bitcast.3) | data formatting | bytes 1572864

commit v4 on v3

--- a/solution.py
+++ b/solution.py
@@ -2,7 +2,6 @@
 
 import jax
 import jax.numpy as jnp
-import numpy as np
 from jax import lax
 from jax.experimental import pallas as pl
 from jax.experimental.pallas import tpu as pltpu
@@ -21,16 +20,6 @@
 ORDER = (4, 3, 5, 2, 6, 1, 7)
 
 
-def tables():
-    sample = np.arange(SIZE)[:, None]
-    odd = 2 * np.arange(SIZE // 2)[None, :] + 1
-    angle = (sample * odd % (2 * SIZE)) * (math.pi / SIZE)
-    forward = np.concatenate([np.cos(angle), -np.sin(angle)], axis=1)
-    weight = 2.0 / SIZE * math.sqrt(WIN)
-    back = weight * forward[:LAGS].T
-    return jnp.asarray(forward, jnp.bfloat16), jnp.asarray(back, jnp.bfloat16)
-
-
 def upper(shape, axis):
     return lax.broadcasted_iota(jnp.int32, shape, axis) < 4
 
@@ -40,9 +29,9 @@
 
 
 def kernel(
-    slots_ref, count_ref, wave_ref, forward_hbm, back_hbm, out_ref,
+    slots_ref, count_ref, wave_ref, out_ref,
     forward_ref, back_ref, raw, parts, held, wide, first_spec, second_spec, nyquist, adder, cross, rank_one,
-    joined, table_sem, raw_sem, own_sem, y_send, y_recv, z_send, z_recv, s_send, s_recv,
+    joined, raw_sem, own_sem, y_send, y_recv, z_send, z_recv, s_send, s_recv,
 ):
     ev = lax.axis_index("ev")
     st = lax.axis_index("st")
@@ -56,13 +45,6 @@
         copy = pltpu.make_async_copy(wave_ref.at[:, c], raw.at[:, c], raw_sem.at[c])
         copy.start()
         raw_copies.append(copy)
-    table_copies = [
-        pltpu.make_async_copy(forward_hbm, forward_ref, table_sem.at[0]),
-        pltpu.make_async_copy(back_hbm, back_ref, table_sem.at[1]),
-    ]
-    for copy in table_copies:
-        copy.start()
-
     barrier = pltpu.get_barrier_semaphore()
     first = lax.rem(ev // 2, COLUMN) == 0
     last = lax.rem(ev // 2, COLUMN) == COLUMN - 1
@@ -143,6 +125,32 @@
             device_id=(ev, lax.rem(st + 1, ST)),
             device_id_type=MESH,
         )
+
+    def make_tables():
+        def turns(rows, step):
+            shape = (rows, SIZE // 2)
+            odd = 2 * lax.broadcasted_iota(jnp.int32, shape, 1) + 1
+            phase = lax.rem(step * lax.broadcasted_iota(jnp.int32, shape, 0) * odd, 2 * SIZE)
+            angle = phase.astype(jnp.float32) * (math.pi / SIZE)
+            return jnp.cos(angle), jnp.sin(angle)
+
+        fine_cos, fine_sin = turns(16, 1)
+        coarse_cos, coarse_sin = turns(SIZE // 16, 16)
+        halves = [[], []]
+        for n in range(SIZE // 16):
+            c, s = coarse_cos[n : n + 1], coarse_sin[n : n + 1]
+            cosine = c * fine_cos - s * fine_sin
+            sine = -(s * fine_cos + c * fine_sin)
+            rows = slice(16 * n, 16 * n + 16)
+            forward_ref[rows, : SIZE // 2] = cosine.astype(jnp.bfloat16)
+            forward_ref[rows, SIZE // 2 :] = sine.astype(jnp.bfloat16)
+            if n < LAGS // 16:
+                halves[0].append(cosine)
+                halves[1].append(sine)
+        weight = 2.0 / SIZE * math.sqrt(WIN)
+        for k, half in enumerate(halves):
+            table = weight * jnp.transpose(jnp.concatenate(half, axis=0))
+            back_ref[k * (SIZE // 2) : (k + 1) * (SIZE // 2), :] = table.astype(jnp.bfloat16)
 
     def lay_out(c):
         def group(g, carry):
@@ -305,8 +313,7 @@
     for n in range(PIECES):
         own_copy(n).wait()
         z_copy(n, rows_of(st)).start()
-    for copy in table_copies:
-        copy.wait()
+    make_tables()
     row = lax.broadcasted_iota(jnp.int32, adder.shape, 0)
     column = lax.broadcasted_iota(jnp.int32, adder.shape, 1)
     sign = 1.0 - 2.0 * lax.rem(row, 2).astype(jnp.float32)
@@ -326,7 +333,6 @@
 
 
 def shards(waveforms, pair_list, pair_count):
-    forward, back = tables()
     windows = jnp.transpose(waveforms, (0, 2, 1, 3))
     slots = jnp.transpose(pair_list, (2, 0, 1))
     whole = pl.BlockSpec(memory_space=pltpu.VMEM)
@@ -336,7 +342,7 @@
     result = pl.pallas_call(
         kernel,
         out_shape=jax.ShapeDtypeStruct((PAIRS, COMP, STATIONS, LAGS), jnp.float32),
-        in_specs=[scalar, scalar, anywhere, anywhere, anywhere],
+        in_specs=[scalar, scalar, anywhere],
         out_specs=whole,
         scratch_shapes=[
             pltpu.VMEM((SIZE, SIZE), jnp.bfloat16),
@@ -352,7 +358,6 @@
             pltpu.VMEM((PAIRS * 8, SIZE), jnp.bfloat16),
             pltpu.VMEM((PAIRS, 8, 128), jnp.float32),
             pltpu.SemaphoreType.REGULAR,
-            dma((2,)),
             dma((COMP,)),
             dma((PIECES,)),
             dma((PIECES,)),
@@ -363,10 +368,10 @@
             dma((PIECES,)),
         ],
         compiler_params=pltpu.CompilerParams(
-            collective_id=0, has_side_effects=True, vmem_limit_bytes=58 * 2**20
+            collective_id=0, has_side_effects=True, vmem_limit_bytes=52 * 2**20
         ),
         name="pair_correlation",
-    )(slots, pair_count, windows, forward, back)
+    )(slots, pair_count, windows)
     return jnp.transpose(result, (0, 2, 1, 3))
 
 

time: 58.2 us -> 56.6 us (0.973)
  Pallas kernels: 54.9 us -> 53.8 us
    pallas_call x1, Pallas kernels: 54.9 us -> 53.8 us  [shards(): pl.pallas_call(kernel, out_shape=jax.ShapeDtypeStruct((PAIRS, COMP, STATI...]
    unnamed x1 -> x3, local copies, waits for them, and re-layouts: 2.09 us -> 1.56 us
where the time goes in v4:
time: 56.6 us; the launch traced here: 56 us
  Pallas kernels  53.8 us (95%)
  local copies, waits for them, and re-layouts  1.56 us (3%)
  between operations  0.67 us (1%)
    pallas_call x1, Pallas kernels, shards(): pl.pallas_call(kernel, out_shape=jax.ShapeDtypeStruct((PAIRS, COMP, STATI...  53.8 us
    unnamed x3, local copies, waits for them, and re-layouts  1.56 us

profile of v4, /device:TPU:1, one launch (start us, length us, event | category | flops | bytes accessed | tf_op | source)
XLA Modules:
  0.0 56.0 jit_solution(2342926493666853103)
XLA Ops:
  0.7 0.0 copy-start
  0.7 0.7 %copy-done = s32[1,64,3]{1,0,2:T(1,128)S(1)} copy-done((s32[1,64,3]{1,0,2:T(1,128)S(1)}, s32[1,64,3]{1,0,2:T(1,128)}, u32[]{:S(2)}) %copy-start) | copy-done | bytes 792
  1.3 53.8 %pair_correlation.1 = f32[64,3,4,256]{3,2,1,0:T(4,128)S(1)} custom-call(s32[3,1,64]{2,1,0:T(1,128)S(1)} %bitcast.4, s32[1]{0:T(128)S(6)} %copy.5.count_ref, bf16[4,3,32,2048]{3,2,1,0:T(8,128)(2,1)} %bitcast.5), custom_call_target="tpu_custom_call" | custom-call | tf_op jit(solution)/shard_map/pair_correlation/pallas_call | solution.py:342
  55.2 0.9 %copy.6 = f32[64,4,3,256]{3,1,2,0:T(4,128)} copy(f32[64,4,3,256]{3,1,2,0:T(4,128)S(1)} %bitcast.3) | data formatting | bytes 1572864
Async XLA Ops:
  0.7 0.7 %copy-start = (s32[1,64,3]{1,0,2:T(1,128)S(1)}, s32[1,64,3]{1,0,2:T(1,128)}, u32[]{:S(2)}) copy-start(s32[1,64,3]{1,0,2:T(1,128)} %param.4) | copy-start | bytes 2308

commit v5 on v4

--- a/solution.py
+++ b/solution.py
@@ -192,12 +192,16 @@
             wide_high = high.astype(jnp.float32)
             rest = jnp.where(jnp.abs(wide_high) < jnp.inf, value - wide_high, 0.0)
             split += [high, rest.astype(jnp.bfloat16)]
-        sums = jnp.dot(
-            jnp.concatenate(split, axis=1), adder[...], preferred_element_type=jnp.float32
-        ).reshape(EVENTS // 2, 8, 256)
-        sums = sums + swap_halves(sums)
-        scale = 1.0 / jnp.sqrt(WIN * (sums[:, :, :128] * (1.0 / WIN) + 1e-6))
-        alternate = sums[:, :, 128:] * scale
+        sums = []
+        for k in range(2):
+            value = jnp.dot(
+                jnp.concatenate(split[2 * k : 2 * k + 2], axis=1),
+                adder[256 * k : 256 * k + 256, 128 * k : 128 * k + 128],
+                preferred_element_type=jnp.float32,
+            ).reshape(EVENTS // 2, 8, 128)
+            sums.append(value + swap_halves(value))
+        scale = 1.0 / jnp.sqrt(WIN * (sums[0] * (1.0 / WIN) + 1e-6))
+        alternate = sums[1] * scale
         for k, events in enumerate(events_of(half, block)):
             nyquist[events] = alternate[2 * k : 2 * k + 2]
         return scale

time: 56.6 us -> 56.6 us (level)
  no operation moved by 1% of the time
where the time goes in v5:
time: 56.6 us; the launch traced here: 56.1 us
  Pallas kernels  53.8 us (95%)
  local copies, waits for them, and re-layouts  1.56 us (3%)
  between operations  0.67 us (1%)
    pallas_call x1, Pallas kernels, shards(): pl.pallas_call(kernel, out_shape=jax.ShapeDtypeStruct((PAIRS, COMP, STATI...  53.8 us
    unnamed x3, local copies, waits for them, and re-layouts  1.56 us

profile of v5, /device:TPU:1, one launch (start us, length us, event | category | flops | bytes accessed | tf_op | source)
XLA Modules:
  0.0 56.1 jit_solution(9626558703156498481)
XLA Ops:
  0.7 0.0 copy-start
  0.7 0.7 %copy-done = s32[1,64,3]{1,0,2:T(1,128)S(1)} copy-done((s32[1,64,3]{1,0,2:T(1,128)S(1)}, s32[1,64,3]{1,0,2:T(1,128)}, u32[]{:S(2)}) %copy-start) | copy-done | bytes 792
  1.3 53.8 %pair_correlation.1 = f32[64,3,4,256]{3,2,1,0:T(4,128)S(1)} custom-call(s32[3,1,64]{2,1,0:T(1,128)S(1)} %bitcast.4, s32[1]{0:T(128)S(6)} %copy.5.count_ref, bf16[4,3,32,2048]{3,2,1,0:T(8,128)(2,1)} %bitcast.5), custom_call_target="tpu_custom_call" | custom-call | tf_op jit(solution)/shard_map/pair_correlation/pallas_call | solution.py:346
  55.2 0.9 %copy.6 = f32[64,4,3,256]{3,1,2,0:T(4,128)} copy(f32[64,4,3,256]{3,1,2,0:T(4,128)S(1)} %bitcast.3) | data formatting | bytes 1572864
Async XLA Ops:
  0.7 0.7 %copy-start = (s32[1,64,3]{1,0,2:T(1,128)S(1)}, s32[1,64,3]{1,0,2:T(1,128)}, u32[]{:S(2)}) copy-start(s32[1,64,3]{1,0,2:T(1,128)} %param.4) | copy-start | bytes 2308
